TPU v7x, 512 devices: a whole 4x4x16 slice. The times are simulated.
512 devices in a mesh: face: 4 (over z_lo), tile: 64 (over y, z_hi, x), lev: 2 (over core).
Axes of the slice: x: 4, y: 4, z: 16 (z_hi: 4, z_lo: 4; z = z_hi * 4 + z_lo), core: 2. Of those that a mesh axis runs over, the one named last changes fastest.
Arguments:
- flux: float32 [2048, 8, 512], P(('face', 'tile')), may hold values from -6 to 6
- profile: float32 [16], P('lev'), may hold values from 0.2 to 1
- courant: float32 [2, 16, 512, 2048], P(None, 'lev', 'tile', 'face'), may hold values from 0.05 to 0.45
- winds: int32 [2, 16, 512, 2048], P(None, 'lev', 'tile', 'face'), may hold values from 0 to 1
- cells: int32 [64, 4, 128], P('tile', 'face'), may hold values from 0 to 4095, as said below
- counts: int32 [64, 4], P('tile', 'face'), may hold values from 32 to 128, as said below
- kernels: float32 [16, 64, 4, 128], P('lev', 'tile', 'face'), may hold values from 0.25 to 0.75
- month_weight: float32 [8, 64, 4, 128], P(None, 'tile', 'face'), may hold values from 0 to 1
- observed: float32 [64, 4, 128], P('tile', 'face'), may hold values from -8 to 8
- obs_weight: float32 [64, 4, 128], P('tile', 'face'), may hold values from 0.5 to 2
- precision: float32 [8], replicated, may hold values from 0.5 to 2
Outputs:
- flux_gradient: float32 [8, 512, 2048], P(None, 'tile', 'face')
- precision_gradient: float32 [8], replicated
Inputs may be any that keep to these rules, and one draw needn't show every extreme that they name: Within each block the 128 entries are distinct cells, numbered row by row over the block's 8 rows of 512 cells; the first four slots of every block hold, in some order, a cell of the block's first column, one of its last column, and interior cells of its first row and of its last row. `counts`: slot s of a block holds a sounding when s is below the block's count; some block is full and some holds exactly 32.
All inputs are finite; a program needn't handle non-finite values.
Results may differ from a plain program's by a relative error of at most 0.00015.
Values sent between devices are 32-bit elements; how exact they have to be, the bound alone decides.
A program may use at most 64 MiB of HBM per device.

v0:
```python
import jax
import jax.numpy as jnp
from jax import lax
from jax.sharding import PartitionSpec as P

KAPPA = 0.025


def extended(x, sides, width, wrap):
    for axis, dim in sides:
        devices, length = (lax.axis_size(axis), x.shape[dim])
        up = [(i, (i + 1) % devices) for i in range(devices if wrap else devices - 1)]
        down = [(j, i) for i, j in up]
        last = lax.slice_in_dim(x, length - width, length, axis=dim)
        initial = lax.slice_in_dim(x, 0, width, axis=dim)
        before = lax.ppermute(last, axis, up)
        after = lax.ppermute(initial, axis, down)
        x = jnp.concatenate([before, x, after], axis=dim)
    return x


def shifted(x, axis, by):
    devices = lax.axis_size(axis)
    return lax.ppermute(x, axis, [(i, (i + by) % devices) for i in range(devices)])


def shifted_2(value, axis, steps):
    count = lax.axis_size(axis)
    initial, last = (max(0, -steps), min(count, count - steps))
    return lax.ppermute(value, axis, [(source, source + steps) for source in range(initial, last)])


def weights_from(speed_x, speed_y, east_flag, north_flag):
    w_west = speed_x * (1.0 - east_flag) + KAPPA
    w_east = speed_x * east_flag + KAPPA
    w_south = speed_y * (1.0 - north_flag) + KAPPA
    w_north = speed_y * north_flag + KAPPA
    w_centre = 1.0 - speed_x - speed_y - 4.0 * KAPPA
    return (w_centre, w_west, w_east, w_south, w_north)


def flags_of(winds):
    return ((winds[0] == 1).astype(jnp.float32), (winds[1] == 1).astype(jnp.float32))


def advance(conc, coeffs):
    w_centre, w_west, w_east, w_south, w_north = coeffs
    side = extended(conc, (("face", 3),), 1, True)
    rim = extended(conc, (("tile", 2),), 1, False)
    return (
        w_centre * conc
        + w_west * side[..., :-2]
        + w_east * side[..., 2:]
        + w_south * rim[..., :-2, :]
        + w_north * rim[..., 2:, :]
    )


def retreat(grad, coeffs):
    w_centre, w_west, w_east, w_south, w_north = coeffs
    west_weighted = w_west * grad
    east_weighted = w_east * grad
    south_weighted = w_south * grad
    north_weighted = w_north * grad
    from_east = shifted(west_weighted[..., :1], "face", -1)
    from_west = shifted(east_weighted[..., -1:], "face", 1)
    from_above = shifted_2(south_weighted[..., :1, :], "tile", -1)
    from_below = shifted_2(north_weighted[..., -1:, :], "tile", 1)
    west_part = jnp.concatenate([west_weighted[..., 1:], from_east], -1)
    east_part = jnp.concatenate([from_west, east_weighted[..., :-1]], -1)
    south_part = jnp.concatenate([south_weighted[..., 1:, :], from_above], -2)
    north_part = jnp.concatenate([from_below, north_weighted[..., :-1, :]], -2)
    return w_centre * grad + west_part + east_part + south_part + north_part


def on_device(
    flux,
    profile,
    courant,
    winds,
    cells,
    counts,
    kernels,
    month_weight,
    observed,
    obs_weight,
    precision,
):
    n_tracer = flux.shape[1]
    n_level = profile.shape[0]
    slot_total = cells.shape[2]
    moved = lax.all_to_all(flux, "tile", split_axis=2, concat_axis=0, tiled=True)
    field = jnp.transpose(moved, (1, 2, 0))
    rows_dev = field.shape[1]
    cols_dev = field.shape[2]
    n_cell = rows_dev * cols_dev
    east_flag, north_flag = flags_of(winds)
    conc = profile[None, :, None, None] * field[:, None]
    coeffs = weights_from(courant[0], courant[1], east_flag, north_flag)
    conc = advance(advance(conc, coeffs), coeffs)
    slot_cells = cells.reshape(slot_total)
    live = jnp.arange(slot_total, dtype=jnp.int32) < counts.reshape(())
    picker = jnp.where(
        live[:, None] & (slot_cells[:, None] == jnp.arange(n_cell, dtype=jnp.int32)[None, :]),
        1.0,
        0.0,
    ).astype(jnp.float32)
    flat = conc.reshape(n_tracer, n_level, n_cell)
    sampled = jnp.einsum("tlc,sc->tls", flat, picker, precision=lax.Precision.HIGHEST)
    kern = kernels.reshape(n_level, slot_total)
    monthly = month_weight.reshape(n_tracer, slot_total)
    partial_model = jnp.sum(kern * jnp.sum(monthly[:, None, :] * sampled, 0), 0)
    model = lax.psum(partial_model, "lev")
    forcing = jnp.where(
        live, obs_weight.reshape(slot_total) * (observed.reshape(slot_total) - model), 0.0
    )
    values = kern[None] * (monthly * forcing[None])[:, None, :]
    lam = jnp.einsum("tls,sc->tlc", values, picker, precision=lax.Precision.HIGHEST)
    lam = lam.reshape(n_tracer, n_level, rows_dev, cols_dev)
    lam = retreat(retreat(lam, coeffs), coeffs)
    adj_part = jnp.sum(profile[None, :, None, None] * lam, 1)
    all_cells = n_cell * lax.axis_size("tile") * lax.axis_size("face")
    adj = lax.psum(adj_part, "lev")
    flux_gradient = precision[:, None, None] * field - adj
    square_sum = lax.psum(jnp.sum(adj * adj, axis=(1, 2)), ("face", "tile"))
    precision_gradient = 0.5 / precision - 0.5 * (square_sum / all_cells) / (precision * precision)
    return (flux_gradient, precision_gradient)


def solution(mesh):
    return jax.shard_map(
        on_device,
        mesh=mesh,
        in_specs=(
            P(("face", "tile"), None, None),
            P("lev"),
            P(None, "lev", "tile", "face"),
            P(None, "lev", "tile", "face"),
            P("tile", "face", None),
            P("tile", "face"),
            P("lev", "tile", "face", None),
            P(None, "tile", "face", None),
            P("tile", "face", None),
            P("tile", "face", None),
            P(),
        ),
        out_specs=(P(None, "tile", "face"), P()),
        check_vma=False,
    )
```

profile of v0, /device:TPU:32, one launch (start us, length us, event | category | flops | bytes accessed | tf_op | source)
XLA Modules:
  0.0 1168.7 jit_solution(5610475102505204907)
XLA Ops:
  7.2 1.7 copy.25
  8.9 1.7 reshape.69
  10.6 20.3 %all-to-all-start = ((f32[64,1,512]{2,1,0:T(1,128)}), f32[64,1,512]{2,1,0:T(1,128)S(1)}, u32[]{:S(2)}, u32[]{:S(2)}) async-start(f32[64,1,512]{2,1,0:T(1,128)} %reshape.69), calls=%async_computation | async-start | bytes 262144 | tf_op jit(solution)/shard_map/all_to_all | solution.py:92
  31.1 20.0 %all-to-all-done = f32[64,1,512]{2,1,0:T(1,128)S(1)} async-done(((f32[64,1,512]{2,1,0:T(1,128)}), f32[64,1,512]{2,1,0:T(1,128)S(1)}, u32[]{:S(2)}, u32[]{:S(2)}) %all-to-all-start) | async-done | bytes 131104 | tf_op jit(solution)/shard_map/all_to_all | solution.py:92
  51.1 0.5 broadcast.82
  51.6 0.9 reduce.1
  52.6 1.1 reshape.70
  53.7 2.4 copy.27
  56.1 2.8 all_to_all.16
  58.9 0.2 broadcast_multiply_fusion.8
  59.1 0.1 fusion.52
  59.3 2.5 collective-permute-start.2
  61.8 1.3 collective-permute-start.3
  63.1 2.9 collective-permute-start
  66.1 2.9 collective-permute-start.1
  69.7 0.1 copy.31
  69.8 0.1 copy.29
  69.9 0.1 copy.30
  70.0 0.1 copy.32
  70.0 0.1 copy.28
  70.1 4.1 collective-permute-done
  74.2 7.7 collective-permute-done.1
  81.9 0.8 fusion.24
  82.7 1.3 collective-permute-start.6
  84.0 1.3 collective-permute-start.7
  85.3 0.1 fusion.50
  85.5 5.5 collective-permute-start.4
  91.0 1.9 collective-permute-start.5
  93.0 7.6 collective-permute-done.4
  100.5 0.8 fusion.16
  101.3 2.4 fusion.12
  103.8 2.6 psum.21
  106.5 1.7 fusion
  108.2 0.6 broadcast_multiply_fusion.5
  108.8 1.3 collective-permute-start.10
  110.1 4.9 collective-permute-start.11
  115.1 0.1 slice.162
  115.2 3.2 collective-permute-start.8
  118.4 3.1 collective-permute-start.9
  121.6 0.1 copy.35
  121.7 0.1 slice.167
  121.7 0.1 slice.164
  121.8 0.3 slice.160
  122.2 3.8 collective-permute-done.8
  126.0 6.6 collective-permute-done.9
  132.5 1.1 broadcast_multiply_fusion.6
  133.6 4.2 collective-permute-start.12
  137.9 0.2 broadcast_multiply_fusion.4
  138.1 0.3 slice.168
  138.6 5.9 collective-permute-start.15
  144.5 1.3 collective-permute-start.14
  145.8 0.1 slice.170
  146.0 3.7 collective-permute-start.13
  149.7 0.2 pad_maximum_fusion.12
  149.8 7.5 collective-permute-done.13
  157.3 0.3 pad_maximum_fusion.13
  157.7 0.1 pad_maximum_fusion.15
  157.8 9.1 collective-permute-done.14
  167.0 1.1 multiply_reduce_fusion
  168.1 0.7 copy.38
  168.8 66.5 %all-reduce.2.cloned.1.call-done = f32[8,8,512]{2,1,0:T(8,128)} async-done(((f32[8,8,512]{2,1,0:T(8,128)}), f32[8,8,512]{2,1,0:T(8,128)}) %all-reduce.2.cloned.1.call-update) | async-done | bytes 131088 | tf_op jit(solution)/shard_map/psum | solution.py:123
  235.3 1.7 multiply_reduce_fusion.1
  237.0 924.4 %psum.23 = f32[8]{0:T(128)S(1)} all-reduce(f32[8]{0:T(128)S(1)} %get-tuple-element.33), channel_id=1, replica_groups=mesh['face'=4,'tile'=64,'lev'=2] {'face','tile'}, use_global_device_ids=true, to_apply=%region_6.7 | all-reduce | flops 8 | bytes 64 | tf_op jit(solution)/shard_map/psum | solution.py:125
  1161.3 0.5 divide_subtract_fusion
  (46 shorter events, 0.6 us)
Async XLA Ops:
  7.2 23.8 %copy-start = (f32[2,8,8,512]{3,2,1,0:T(8,128)S(1)}, f32[2,8,8,512]{3,2,1,0:T(8,128)}, u32[]{:S(2)}) copy-start(f32[2,8,8,512]{3,2,1,0:T(8,128)} %param.13) | copy-start | bytes 786436
  7.2 23.8 %copy-start.1 = (s32[2,8,8,512]{3,2,1,0:T(8,128)S(1)}, s32[2,8,8,512]{3,2,1,0:T(8,128)}, u32[]{:S(2)}) copy-start(s32[2,8,8,512]{3,2,1,0:T(8,128)} %param.14) | copy-start | bytes 786436
  10.6 40.5 %all-to-all-start = ((f32[64,1,512]{2,1,0:T(1,128)}), f32[64,1,512]{2,1,0:T(1,128)S(1)}, u32[]{:S(2)}, u32[]{:S(2)}) async-start(f32[64,1,512]{2,1,0:T(1,128)} %reshape.69), calls=%async_computation | async-start | bytes 262144 | tf_op jit(solution)/shard_map/all_to_all | solution.py:92
  30.9 204.3 %all-reduce.2.cloned.1.call-start = ((), (), s32[]{:S(2)}) async-start(), calls=%async_computation.1 | async-start | bytes 262144 | tf_op jit(solution)/shard_map/psum | solution.py:123
  56.1 2.8 copy-start.4
  59.3 22.6 %collective-permute-start.2 = (f32[8,8,1,512]{3,1,2,0:T(8,128)S(1)}, f32[8,8,1,512]{3,1,2,0:T(8,128)S(1)}, u32[]{:S(2)}, u32[]{:S(2)}) collective-permute-start(f32[8,8,1,512]{3,1,2,0:T(8,128)S(1)} %get-tuple-element.25), channel_id=1, source_target_pairs={{0,2},{2,4},{4,6},{6,8},{8,10},{10,12},{12,14},{14,16},{16,18},{18... | collective-permute-start | bytes 393224 | tf_op jit(solution)/shard_map/ppermute | solution.py:16
  61.8 20.1 %collective-permute-start.3 = (f32[8,8,1,512]{3,1,2,0:T(8,128)S(1)}, f32[8,8,1,512]{3,1,2,0:T(8,128)S(1)}, u32[]{:S(2)}, u32[]{:S(2)}) collective-permute-start(f32[8,8,1,512]{3,1,2,0:T(8,128)S(1)} %get-tuple-element.26), channel_id=1, source_target_pairs={{2,0},{4,2},{6,4},{8,6},{10,8},{12,10},{14,12},{16,14},{18,16},{20... | collective-permute-start | bytes 393224 | tf_op jit(solution)/shard_map/ppermute | solution.py:17
  63.1 11.1 collective-permute-start
  66.1 15.9 %collective-permute-start.1 = (f32[8,8,8,1]{3,1,2,0:T(8,128)S(1)}, f32[8,8,8,1]{3,1,2,0:T(8,128)S(1)}, u32[]{:S(2)}, u32[]{:S(2)}) collective-permute-start(f32[8,8,8,1]{3,1,2,0:T(8,128)S(1)} %get-tuple-element.24), channel_id=1, source_target_pairs={{128,0},{256,128},{384,256},{0,384},{129,1},{257,129},{385,257},{1... | collective-permute-start | bytes 6152 | tf_op jit(solution)/shard_map/ppermute | solution.py:17
  82.7 17.8 %collective-permute-start.6 = (f32[8,8,1,512]{3,1,2,0:T(8,128)S(1)}, f32[8,8,1,512]{3,1,2,0:T(8,128)S(1)}, u32[]{:S(2)}, u32[]{:S(2)}) collective-permute-start(f32[8,8,1,512]{3,1,2,0:T(8,128)S(1)} %get-tuple-element.21), channel_id=1, source_target_pairs={{0,2},{2,4},{4,6},{6,8},{8,10},{10,12},{12,14},{14,16},{16,18},{18... | collective-permute-start | bytes 393224 | tf_op jit(solution)/shard_map/ppermute | solution.py:16
  84.0 17.3 %copy-start.2 = (f32[8,1,1,128]{3,2,1,0:T(1,128)S(1)}, f32[8,1,1,128]{3,2,1,0:T(1,128)}, u32[]{:S(2)}) copy-start(f32[8,1,1,128]{3,2,1,0:T(1,128)} %param.18) | copy-start | bytes 12292
  84.0 17.3 %copy-start.8 = (s32[1,1,128]{2,1,0:T(1,128)S(1)}, s32[1,1,128]{2,1,0:T(1,128)}, u32[]{:S(2)}) copy-start(s32[1,1,128]{2,1,0:T(1,128)} %param.15) | copy-start | bytes 1540
  84.0 16.5 %collective-permute-start.7 = (f32[8,8,1,512]{3,1,2,0:T(8,128)S(1)}, f32[8,8,1,512]{3,1,2,0:T(8,128)S(1)}, u32[]{:S(2)}, u32[]{:S(2)}) collective-permute-start(f32[8,8,1,512]{3,1,2,0:T(8,128)S(1)} %get-tuple-element.22), channel_id=1, source_target_pairs={{2,0},{4,2},{6,4},{8,6},{10,8},{12,10},{14,12},{16,14},{18,16},{20... | collective-permute-start | bytes 393224 | tf_op jit(solution)/shard_map/ppermute | solution.py:17
  85.5 15.0 %collective-permute-start.4 = (f32[8,8,8,1]{3,1,2,0:T(8,128)S(1)}, f32[8,8,8,1]{3,1,2,0:T(8,128)S(1)}, u32[]{:S(2)}, u32[]{:S(2)}) collective-permute-start(f32[8,8,8,1]{3,1,2,0:T(8,128)S(1)} %get-tuple-element.19), channel_id=1, source_target_pairs={{0,128},{128,256},{256,384},{384,0},{1,129},{129,257},{257,385},{3... | collective-permute-start | bytes 6152 | tf_op jit(solution)/shard_map/ppermute | solution.py:16
  91.0 9.6 collective-permute-start.5
  92.9 10.9 copy-start.3
  92.9 13.5 %copy-start.6 = (f32[1,1,128]{2,1,0:T(1,128)S(1)}, f32[1,1,128]{2,1,0:T(1,128)}, u32[]{:S(2)}) copy-start(f32[1,1,128]{2,1,0:T(1,128)} %param.19) | copy-start | bytes 1540
  92.9 13.5 %copy-start.7 = (f32[1,1,128]{2,1,0:T(1,128)S(1)}, f32[1,1,128]{2,1,0:T(1,128)}, u32[]{:S(2)}) copy-start(f32[1,1,128]{2,1,0:T(1,128)} %param.20) | copy-start | bytes 1540
  108.8 23.7 %collective-permute-start.10 = (f32[8,8,1,512]{3,1,2,0:T(8,128)S(1)}, f32[8,8,1,512]{3,1,2,0:T(8,128)S(1)}, u32[]{:S(2)}, u32[]{:S(2)}) collective-permute-start(f32[8,8,1,512]{3,1,2,0:T(8,128)S(1)} %slice.165), channel_id=1, source_target_pairs={{2,0},{4,2},{6,4},{8,6},{10,8},{12,10},{14,12},{16,14},{18,16},{20... | collective-permute-start | bytes 393224 | tf_op jit(solution)/shard_map/ppermute | solution.py:30
  110.1 22.4 %collective-permute-start.11 = (f32[8,8,1,512]{3,1,2,0:T(8,128)S(1)}, f32[8,8,1,512]{3,1,2,0:T(8,128)S(1)}, u32[]{:S(2)}, u32[]{:S(2)}) collective-permute-start(f32[8,8,1,512]{3,1,2,0:T(8,128)S(1)} %slice.166), channel_id=1, source_target_pairs={{0,2},{2,4},{4,6},{6,8},{8,10},{10,12},{12,14},{14,16},{16,18},{18... | collective-permute-start | bytes 393224 | tf_op jit(solution)/shard_map/ppermute | solution.py:30
  115.2 10.7 collective-permute-start.8
  118.4 14.1 %collective-permute-start.9 = (f32[8,8,8,1]{3,1,2,0:T(8,128)S(1)}, f32[8,8,8,1]{3,1,2,0:T(8,128)S(1)}, u32[]{:S(2)}, u32[]{:S(2)}) collective-permute-start(f32[8,8,8,1]{3,1,2,0:T(8,128)S(1)} %slice.162), channel_id=1, source_target_pairs={{0,128},{128,256},{256,384},{384,0},{1,129},{129,257},{257,385},{3... | collective-permute-start | bytes 6152 | tf_op jit(solution)/shard_map/ppermute | solution.py:24
  133.6 16.0 %collective-permute-start.12 = (f32[8,8,8,1]{3,1,2,0:T(8,128)S(1)}, f32[8,8,8,1]{3,1,2,0:T(8,128)S(1)}, u32[]{:S(2)}, u32[]{:S(2)}) collective-permute-start(f32[8,8,8,1]{3,1,2,0:T(8,128)S(1)} %slice.169), channel_id=1, source_target_pairs={{0,384},{128,0},{256,128},{384,256},{1,385},{129,1},{257,129},{385... | collective-permute-start | bytes 6152 | tf_op jit(solution)/shard_map/ppermute | solution.py:24
  138.6 19.1 %collective-permute-start.15 = (f32[8,8,1,512]{3,1,2,0:T(8,128)S(1)}, f32[8,8,1,512]{3,1,2,0:T(8,128)S(1)}, u32[]{:S(2)}, u32[]{:S(2)}) collective-permute-start(f32[8,8,1,512]{3,1,2,0:T(8,128)S(1)} %slice.174), channel_id=1, source_target_pairs={{0,2},{2,4},{4,6},{6,8},{8,10},{10,12},{12,14},{14,16},{16,18},{18... | collective-permute-start | bytes 393224 | tf_op jit(solution)/shard_map/ppermute | solution.py:30
  144.5 22.3 %collective-permute-start.14 = (f32[8,8,1,512]{3,1,2,0:T(8,128)S(1)}, f32[8,8,1,512]{3,1,2,0:T(8,128)S(1)}, u32[]{:S(2)}, u32[]{:S(2)}) collective-permute-start(f32[8,8,1,512]{3,1,2,0:T(8,128)S(1)} %slice.173), channel_id=1, source_target_pairs={{2,0},{4,2},{6,4},{8,6},{10,8},{12,10},{14,12},{16,14},{18,16},{20... | collective-permute-start | bytes 393224 | tf_op jit(solution)/shard_map/ppermute | solution.py:30
  146.0 11.4 collective-permute-start.13
  166.9 68.3 %copy-start.5 = (f32[8]{0:T(128)S(1)}, f32[8]{0:T(128)}, u32[]{:S(2)}) copy-start(f32[8]{0:T(128)} %param.21) | copy-start | bytes 100
Sparse Core Ops, SparseCore 0:
  169.0 66.2 all-reduce.1
where the time goes:
time: 1170 us
  blocking collectives  927 us (79%)
  waiting for transfers between devices  133 us (11%)
  starting transfers between devices  67.6 us (6%)
  between operations  15.2 us (1%)
  local copies, waits for them, and re-layouts  13.2 us (1%)
    psum x1, blocking collectives, on_device(): square_sum = lax.psum(jnp.sum(adj * adj, axis=(1, 2)), ('face', 'tile'))  924 us
    psum x1, waiting for transfers between devices, on_device(): adj = lax.psum(adj_part, 'lev')  66.5 us
  transfers between devices with their start and end apart: 18, of which 9 were waited for; matrix products, arithmetic and copies ran while one was open for 0% of the time, Pallas kernels for 0%

commit v1 on v0

--- a/solution.py
+++ b/solution.py
@@ -122,7 +122,9 @@
     all_cells = n_cell * lax.axis_size("tile") * lax.axis_size("face")
     adj = lax.psum(adj_part, "lev")
     flux_gradient = precision[:, None, None] * field - adj
-    square_sum = lax.psum(jnp.sum(adj * adj, axis=(1, 2)), ("face", "tile"))
+    square_sum = jnp.sum(adj * adj, axis=(1, 2))
+    for mesh_axis in ("tile", "face"):
+        square_sum = lax.psum(square_sum, mesh_axis)
     precision_gradient = 0.5 / precision - 0.5 * (square_sum / all_cells) / (precision * precision)
     return (flux_gradient, precision_gradient)
 

time: 1170 us -> 480 us (0.41)
  blocking collectives: 927 us -> 237 us
    psum x1 -> x2, blocking collectives: 924 us -> 235 us  [on_device(): square_sum = lax.psum(square_sum, mesh_axis)]
  transfers between devices with their start and end apart: 18 -> 18, of which waited for: 9 -> 9; matrix products, arithmetic and copies ran while one was open for 0% -> 1% of each run, Pallas kernels for 0% -> 0%
where the time goes in v1:
time: 480 us; the launch traced here: 479 us
  blocking collectives  237 us (49%)
  waiting for transfers between devices  133 us (28%)
  starting transfers between devices  67.6 us (14%)
  between operations  15.2 us (3%)
  local copies, waits for them, and re-layouts  13.2 us (3%)
  other arithmetic  8.64 us (2%)
    psum x2, blocking collectives, on_device(): square_sum = lax.psum(square_sum, mesh_axis)  235 us
    psum x1, waiting for transfers between devices, on_device(): adj = lax.psum(adj_part, 'lev')  66.4 us
    all_to_all x1, starting transfers between devices, on_device(): lax.all_to_all(flux, 'tile', split_axis=2, concat_axis=0, tiled=True)  20.3 us
    all_to_all x1, waiting for transfers between devices, on_device(): lax.all_to_all(flux, 'tile', split_axis=2, concat_axis=0, tiled=True)  20 us
    ppermute x4, waiting for transfers between devices, shifted(): lax.ppermute(x, axis, [(i, (i + by) % devices) for i in range(devices)])  17.9 us
    ppermute x4, starting transfers between devices, shifted(): lax.ppermute(x, axis, [(i, (i + by) % devices) for i in range(devices)])  14.3 us
    ppermute x4, starting transfers between devices, shifted_2(): lax.ppermute(value, axis, [(source, source + steps) for source in range(i...  13.4 us
    ppermute x4, starting transfers between devices, extended(): before = lax.ppermute(last, axis, up)  12.2 us
  transfers between devices with their start and end apart: 18, of which 9 were waited for; matrix products, arithmetic and copies ran while one was open for 1% of the time, Pallas kernels for 0%

profile of v1, /device:TPU:32, one launch (start us, length us, event | category | flops | bytes accessed | tf_op | source)
XLA Modules:
  0.0 479.2 jit_solution(5228826029167741256)
XLA Ops:
  7.2 1.7 copy.25
  8.9 1.7 reshape.69
  10.6 20.3 %all-to-all-start = ((f32[64,1,512]{2,1,0:T(1,128)}), f32[64,1,512]{2,1,0:T(1,128)S(1)}, u32[]{:S(2)}, u32[]{:S(2)}) async-start(f32[64,1,512]{2,1,0:T(1,128)} %reshape.69), calls=%async_computation | async-start | bytes 262144 | tf_op jit(solution)/shard_map/all_to_all | solution.py:92
  31.1 20.0 %all-to-all-done = f32[64,1,512]{2,1,0:T(1,128)S(1)} async-done(((f32[64,1,512]{2,1,0:T(1,128)}), f32[64,1,512]{2,1,0:T(1,128)S(1)}, u32[]{:S(2)}, u32[]{:S(2)}) %all-to-all-start) | async-done | bytes 131104 | tf_op jit(solution)/shard_map/all_to_all | solution.py:92
  51.1 0.5 broadcast.82
  51.6 0.9 reduce.1
  52.6 1.1 reshape.70
  53.7 2.4 copy.27
  56.1 2.8 all_to_all.16
  58.9 0.2 broadcast_multiply_fusion.8
  59.1 0.1 fusion.52
  59.3 2.5 collective-permute-start.2
  61.8 1.3 collective-permute-start.3
  63.1 2.9 collective-permute-start
  66.1 2.9 collective-permute-start.1
  69.7 0.1 copy.31
  69.8 0.1 copy.29
  69.9 0.1 copy.30
  69.9 0.1 copy.32
  70.0 0.1 copy.28
  70.1 4.1 collective-permute-done
  74.2 7.7 %collective-permute-done.1 = f32[8,8,8,1]{3,1,2,0:T(8,128)S(1)} collective-permute-done((f32[8,8,8,1]{3,1,2,0:T(8,128)S(1)}, f32[8,8,8,1]{3,1,2,0:T(8,128)S(1)}, u32[]{:S(2)}, u32[]{:S(2)}) %collective-permute-start.1) | collective-permute-done | bytes 2080 | tf_op jit(solution)/shard_map/ppermute | solution.py:17
  81.9 0.8 fusion.24
  82.7 1.3 collective-permute-start.6
  84.0 1.3 collective-permute-start.7
  85.3 0.1 fusion.50
  85.5 5.5 %collective-permute-start.4 = (f32[8,8,8,1]{3,1,2,0:T(8,128)S(1)}, f32[8,8,8,1]{3,1,2,0:T(8,128)S(1)}, u32[]{:S(2)}, u32[]{:S(2)}) collective-permute-start(f32[8,8,8,1]{3,1,2,0:T(8,128)S(1)} %get-tuple-element.19), channel_id=1, source_target_pairs={{0,128},{128,256},{256,384},{384,0},{1,129},{129,257},{257,385},{3... | collective-permute-start | bytes 6152 | tf_op jit(solution)/shard_map/ppermute | solution.py:16
  91.0 1.9 collective-permute-start.5
  93.0 7.6 %collective-permute-done.4 = f32[8,8,8,1]{3,1,2,0:T(8,128)S(1)} collective-permute-done((f32[8,8,8,1]{3,1,2,0:T(8,128)S(1)}, f32[8,8,8,1]{3,1,2,0:T(8,128)S(1)}, u32[]{:S(2)}, u32[]{:S(2)}) %collective-permute-start.4) | collective-permute-done | bytes 2080 | tf_op jit(solution)/shard_map/ppermute | solution.py:16
  100.5 0.8 fusion.16
  101.3 2.5 fusion.12
  103.8 2.6 psum.28
  106.5 1.7 fusion
  108.2 0.6 broadcast_multiply_fusion.5
  108.8 1.3 collective-permute-start.10
  110.1 4.9 %collective-permute-start.11 = (f32[8,8,1,512]{3,1,2,0:T(8,128)S(1)}, f32[8,8,1,512]{3,1,2,0:T(8,128)S(1)}, u32[]{:S(2)}, u32[]{:S(2)}) collective-permute-start(f32[8,8,1,512]{3,1,2,0:T(8,128)S(1)} %slice.166), channel_id=1, source_target_pairs={{0,2},{2,4},{4,6},{6,8},{8,10},{10,12},{12,14},{14,16},{16,18},{18... | collective-permute-start | bytes 393224 | tf_op jit(solution)/shard_map/ppermute | solution.py:30
  115.0 0.1 slice.162
  115.2 3.2 collective-permute-start.8
  118.4 3.1 collective-permute-start.9
  121.6 0.1 copy.35
  121.7 0.1 slice.164
  121.8 0.3 slice.160
  122.2 3.8 collective-permute-done.8
  126.0 6.6 %collective-permute-done.9 = f32[8,8,8,1]{3,1,2,0:T(8,128)S(1)} collective-permute-done((f32[8,8,8,1]{3,1,2,0:T(8,128)S(1)}, f32[8,8,8,1]{3,1,2,0:T(8,128)S(1)}, u32[]{:S(2)}, u32[]{:S(2)}) %collective-permute-start.9) | collective-permute-done | bytes 2080 | tf_op jit(solution)/shard_map/ppermute | solution.py:24
  132.5 1.1 broadcast_multiply_fusion.6
  133.6 4.2 collective-permute-start.12
  137.9 0.2 broadcast_multiply_fusion.4
  138.1 0.3 slice.168
  138.6 5.9 %collective-permute-start.15 = (f32[8,8,1,512]{3,1,2,0:T(8,128)S(1)}, f32[8,8,1,512]{3,1,2,0:T(8,128)S(1)}, u32[]{:S(2)}, u32[]{:S(2)}) collective-permute-start(f32[8,8,1,512]{3,1,2,0:T(8,128)S(1)} %slice.174), channel_id=1, source_target_pairs={{0,2},{2,4},{4,6},{6,8},{8,10},{10,12},{12,14},{14,16},{16,18},{18... | collective-permute-start | bytes 393224 | tf_op jit(solution)/shard_map/ppermute | solution.py:30
  144.5 1.3 collective-permute-start.14
  145.8 0.1 slice.170
  146.0 3.7 collective-permute-start.13
  149.7 0.2 pad_maximum_fusion.12
  149.8 7.5 %collective-permute-done.13 = f32[8,8,8,1]{3,1,2,0:T(8,128)S(1)} collective-permute-done((f32[8,8,8,1]{3,1,2,0:T(8,128)S(1)}, f32[8,8,8,1]{3,1,2,0:T(8,128)S(1)}, u32[]{:S(2)}, u32[]{:S(2)}) %collective-permute-start.13) | collective-permute-done | bytes 2080 | tf_op jit(solution)/shard_map/ppermute | solution.py:24
  157.3 0.3 pad_maximum_fusion.13
  157.7 0.1 pad_maximum_fusion.15
  157.8 9.1 %collective-permute-done.14 = f32[8,8,1,512]{3,1,2,0:T(8,128)S(1)} collective-permute-done((f32[8,8,1,512]{3,1,2,0:T(8,128)S(1)}, f32[8,8,1,512]{3,1,2,0:T(8,128)S(1)}, u32[]{:S(2)}, u32[]{:S(2)}) %collective-permute-start.14) | collective-permute-done | bytes 131104 | tf_op jit(solution)/shard_map/ppermute | solution.py:30
  167.0 1.1 multiply_reduce_fusion
  168.1 0.7 copy.38
  168.8 66.4 %all-reduce.2.cloned.1.call-done = f32[8,8,512]{2,1,0:T(8,128)} async-done(((f32[8,8,512]{2,1,0:T(8,128)}), f32[8,8,512]{2,1,0:T(8,128)}) %all-reduce.2.cloned.1.call-update) | async-done | bytes 131088 | tf_op jit(solution)/shard_map/psum | solution.py:123
  235.3 1.7 multiply_reduce_fusion.1
  237.0 224.8 %psum.30 = f32[8]{0:T(128)S(1)} all-reduce(f32[8]{0:T(128)S(1)} %get-tuple-element.33), channel_id=1, replica_groups=mesh['face'=4,'tile'=64,'lev'=2] {'tile'}, use_global_device_ids=true, to_apply=%region_6.7 | all-reduce | flops 8 | bytes 64 | tf_op jit(solution)/shard_map/psum | solution.py:127
  461.8 10.0 %psum.31 = f32[8]{0:T(128)S(1)} all-reduce(f32[8]{0:T(128)S(1)} %psum.30), channel_id=1, replica_groups=mesh['face'=4,'tile'=64,'lev'=2] {'face'}, use_global_device_ids=true, to_apply=%region_7.8 | all-reduce | flops 8 | bytes 64 | tf_op jit(solution)/shard_map/psum | solution.py:127
  471.8 0.5 divide_subtract_fusion
  (47 shorter events, 0.7 us)
Async XLA Ops:
  7.2 23.8 %copy-start = (f32[2,8,8,512]{3,2,1,0:T(8,128)S(1)}, f32[2,8,8,512]{3,2,1,0:T(8,128)}, u32[]{:S(2)}) copy-start(f32[2,8,8,512]{3,2,1,0:T(8,128)} %param.13) | copy-start | bytes 786436
  7.2 23.8 %copy-start.1 = (s32[2,8,8,512]{3,2,1,0:T(8,128)S(1)}, s32[2,8,8,512]{3,2,1,0:T(8,128)}, u32[]{:S(2)}) copy-start(s32[2,8,8,512]{3,2,1,0:T(8,128)} %param.14) | copy-start | bytes 786436
  10.6 40.5 %all-to-all-start = ((f32[64,1,512]{2,1,0:T(1,128)}), f32[64,1,512]{2,1,0:T(1,128)S(1)}, u32[]{:S(2)}, u32[]{:S(2)}) async-start(f32[64,1,512]{2,1,0:T(1,128)} %reshape.69), calls=%async_computation | async-start | bytes 262144 | tf_op jit(solution)/shard_map/all_to_all | solution.py:92
  30.9 204.3 %all-reduce.2.cloned.1.call-start = ((), (), s32[]{:S(2)}) async-start(), calls=%async_computation.1 | async-start | bytes 262144 | tf_op jit(solution)/shard_map/psum | solution.py:123
  56.1 2.8 copy-start.4
  59.3 22.6 %collective-permute-start.2 = (f32[8,8,1,512]{3,1,2,0:T(8,128)S(1)}, f32[8,8,1,512]{3,1,2,0:T(8,128)S(1)}, u32[]{:S(2)}, u32[]{:S(2)}) collective-permute-start(f32[8,8,1,512]{3,1,2,0:T(8,128)S(1)} %get-tuple-element.25), channel_id=1, source_target_pairs={{0,2},{2,4},{4,6},{6,8},{8,10},{10,12},{12,14},{14,16},{16,18},{18... | collective-permute-start | bytes 393224 | tf_op jit(solution)/shard_map/ppermute | solution.py:16
  61.8 20.1 %collective-permute-start.3 = (f32[8,8,1,512]{3,1,2,0:T(8,128)S(1)}, f32[8,8,1,512]{3,1,2,0:T(8,128)S(1)}, u32[]{:S(2)}, u32[]{:S(2)}) collective-permute-start(f32[8,8,1,512]{3,1,2,0:T(8,128)S(1)} %get-tuple-element.26), channel_id=1, source_target_pairs={{2,0},{4,2},{6,4},{8,6},{10,8},{12,10},{14,12},{16,14},{18,16},{20... | collective-permute-start | bytes 393224 | tf_op jit(solution)/shard_map/ppermute | solution.py:17
  63.1 11.1 %collective-permute-start = (f32[8,8,8,1]{3,1,2,0:T(8,128)S(1)}, f32[8,8,8,1]{3,1,2,0:T(8,128)S(1)}, u32[]{:S(2)}, u32[]{:S(2)}) collective-permute-start(f32[8,8,8,1]{3,1,2,0:T(8,128)S(1)} %get-tuple-element.23), channel_id=1, source_target_pairs={{0,128},{128,256},{256,384},{384,0},{1,129},{129,257},{257,385},{3... | collective-permute-start | bytes 6152 | tf_op jit(solution)/shard_map/ppermute | solution.py:16
  66.1 15.9 %collective-permute-start.1 = (f32[8,8,8,1]{3,1,2,0:T(8,128)S(1)}, f32[8,8,8,1]{3,1,2,0:T(8,128)S(1)}, u32[]{:S(2)}, u32[]{:S(2)}) collective-permute-start(f32[8,8,8,1]{3,1,2,0:T(8,128)S(1)} %get-tuple-element.24), channel_id=1, source_target_pairs={{128,0},{256,128},{384,256},{0,384},{129,1},{257,129},{385,257},{1... | collective-permute-start | bytes 6152 | tf_op jit(solution)/shard_map/ppermute | solution.py:17
  82.7 17.8 %collective-permute-start.6 = (f32[8,8,1,512]{3,1,2,0:T(8,128)S(1)}, f32[8,8,1,512]{3,1,2,0:T(8,128)S(1)}, u32[]{:S(2)}, u32[]{:S(2)}) collective-permute-start(f32[8,8,1,512]{3,1,2,0:T(8,128)S(1)} %get-tuple-element.21), channel_id=1, source_target_pairs={{0,2},{2,4},{4,6},{6,8},{8,10},{10,12},{12,14},{14,16},{16,18},{18... | collective-permute-start | bytes 393224 | tf_op jit(solution)/shard_map/ppermute | solution.py:16
  84.0 17.3 %copy-start.2 = (f32[8,1,1,128]{3,2,1,0:T(1,128)S(1)}, f32[8,1,1,128]{3,2,1,0:T(1,128)}, u32[]{:S(2)}) copy-start(f32[8,1,1,128]{3,2,1,0:T(1,128)} %param.18) | copy-start | bytes 12292
  84.0 17.3 %copy-start.8 = (s32[1,1,128]{2,1,0:T(1,128)S(1)}, s32[1,1,128]{2,1,0:T(1,128)}, u32[]{:S(2)}) copy-start(s32[1,1,128]{2,1,0:T(1,128)} %param.15) | copy-start | bytes 1540
  84.0 16.5 %collective-permute-start.7 = (f32[8,8,1,512]{3,1,2,0:T(8,128)S(1)}, f32[8,8,1,512]{3,1,2,0:T(8,128)S(1)}, u32[]{:S(2)}, u32[]{:S(2)}) collective-permute-start(f32[8,8,1,512]{3,1,2,0:T(8,128)S(1)} %get-tuple-element.22), channel_id=1, source_target_pairs={{2,0},{4,2},{6,4},{8,6},{10,8},{12,10},{14,12},{16,14},{18,16},{20... | collective-permute-start | bytes 393224 | tf_op jit(solution)/shard_map/ppermute | solution.py:17
  85.5 15.0 %collective-permute-start.4 = (f32[8,8,8,1]{3,1,2,0:T(8,128)S(1)}, f32[8,8,8,1]{3,1,2,0:T(8,128)S(1)}, u32[]{:S(2)}, u32[]{:S(2)}) collective-permute-start(f32[8,8,8,1]{3,1,2,0:T(8,128)S(1)} %get-tuple-element.19), channel_id=1, source_target_pairs={{0,128},{128,256},{256,384},{384,0},{1,129},{129,257},{257,385},{3... | collective-permute-start | bytes 6152 | tf_op jit(solution)/shard_map/ppermute | solution.py:16
  91.0 9.6 %collective-permute-start.5 = (f32[8,8,8,1]{3,1,2,0:T(8,128)S(1)}, f32[8,8,8,1]{3,1,2,0:T(8,128)S(1)}, u32[]{:S(2)}, u32[]{:S(2)}) collective-permute-start(f32[8,8,8,1]{3,1,2,0:T(8,128)S(1)} %get-tuple-element.20), channel_id=1, source_target_pairs={{128,0},{256,128},{384,256},{0,384},{129,1},{257,129},{385,257},{1... | collective-permute-start | bytes 6152 | tf_op jit(solution)/shard_map/ppermute | solution.py:17
  92.9 10.9 %copy-start.3 = (f32[8,1,1,128]{3,2,1,0:T(1,128)S(1)}, f32[8,1,1,128]{3,2,1,0:T(1,128)}, u32[]{:S(2)}) copy-start(f32[8,1,1,128]{3,2,1,0:T(1,128)} %param.17) | copy-start | bytes 12292
  92.9 13.5 %copy-start.6 = (f32[1,1,128]{2,1,0:T(1,128)S(1)}, f32[1,1,128]{2,1,0:T(1,128)}, u32[]{:S(2)}) copy-start(f32[1,1,128]{2,1,0:T(1,128)} %param.19) | copy-start | bytes 1540
  92.9 13.5 %copy-start.7 = (f32[1,1,128]{2,1,0:T(1,128)S(1)}, f32[1,1,128]{2,1,0:T(1,128)}, u32[]{:S(2)}) copy-start(f32[1,1,128]{2,1,0:T(1,128)} %param.20) | copy-start | bytes 1540
  108.8 23.7 %collective-permute-start.10 = (f32[8,8,1,512]{3,1,2,0:T(8,128)S(1)}, f32[8,8,1,512]{3,1,2,0:T(8,128)S(1)}, u32[]{:S(2)}, u32[]{:S(2)}) collective-permute-start(f32[8,8,1,512]{3,1,2,0:T(8,128)S(1)} %slice.165), channel_id=1, source_target_pairs={{2,0},{4,2},{6,4},{8,6},{10,8},{12,10},{14,12},{16,14},{18,16},{20... | collective-permute-start | bytes 393224 | tf_op jit(solution)/shard_map/ppermute | solution.py:30
  110.1 22.4 %collective-permute-start.11 = (f32[8,8,1,512]{3,1,2,0:T(8,128)S(1)}, f32[8,8,1,512]{3,1,2,0:T(8,128)S(1)}, u32[]{:S(2)}, u32[]{:S(2)}) collective-permute-start(f32[8,8,1,512]{3,1,2,0:T(8,128)S(1)} %slice.166), channel_id=1, source_target_pairs={{0,2},{2,4},{4,6},{6,8},{8,10},{10,12},{12,14},{14,16},{16,18},{18... | collective-permute-start | bytes 393224 | tf_op jit(solution)/shard_map/ppermute | solution.py:30
  115.2 10.7 %collective-permute-start.8 = (f32[8,8,8,1]{3,1,2,0:T(8,128)S(1)}, f32[8,8,8,1]{3,1,2,0:T(8,128)S(1)}, u32[]{:S(2)}, u32[]{:S(2)}) collective-permute-start(f32[8,8,8,1]{3,1,2,0:T(8,128)S(1)} %slice.161), channel_id=1, source_target_pairs={{0,384},{128,0},{256,128},{384,256},{1,385},{129,1},{257,129},{385... | collective-permute-start | bytes 6152 | tf_op jit(solution)/shard_map/ppermute | solution.py:24
  118.4 14.1 %collective-permute-start.9 = (f32[8,8,8,1]{3,1,2,0:T(8,128)S(1)}, f32[8,8,8,1]{3,1,2,0:T(8,128)S(1)}, u32[]{:S(2)}, u32[]{:S(2)}) collective-permute-start(f32[8,8,8,1]{3,1,2,0:T(8,128)S(1)} %slice.162), channel_id=1, source_target_pairs={{0,128},{128,256},{256,384},{384,0},{1,129},{129,257},{257,385},{3... | collective-permute-start | bytes 6152 | tf_op jit(solution)/shard_map/ppermute | solution.py:24
  133.6 16.0 %collective-permute-start.12 = (f32[8,8,8,1]{3,1,2,0:T(8,128)S(1)}, f32[8,8,8,1]{3,1,2,0:T(8,128)S(1)}, u32[]{:S(2)}, u32[]{:S(2)}) collective-permute-start(f32[8,8,8,1]{3,1,2,0:T(8,128)S(1)} %slice.169), channel_id=1, source_target_pairs={{0,384},{128,0},{256,128},{384,256},{1,385},{129,1},{257,129},{385... | collective-permute-start | bytes 6152 | tf_op jit(solution)/shard_map/ppermute | solution.py:24
  138.6 19.1 %collective-permute-start.15 = (f32[8,8,1,512]{3,1,2,0:T(8,128)S(1)}, f32[8,8,1,512]{3,1,2,0:T(8,128)S(1)}, u32[]{:S(2)}, u32[]{:S(2)}) collective-permute-start(f32[8,8,1,512]{3,1,2,0:T(8,128)S(1)} %slice.174), channel_id=1, source_target_pairs={{0,2},{2,4},{4,6},{6,8},{8,10},{10,12},{12,14},{14,16},{16,18},{18... | collective-permute-start | bytes 393224 | tf_op jit(solution)/shard_map/ppermute | solution.py:30
  144.5 22.3 %collective-permute-start.14 = (f32[8,8,1,512]{3,1,2,0:T(8,128)S(1)}, f32[8,8,1,512]{3,1,2,0:T(8,128)S(1)}, u32[]{:S(2)}, u32[]{:S(2)}) collective-permute-start(f32[8,8,1,512]{3,1,2,0:T(8,128)S(1)} %slice.173), channel_id=1, source_target_pairs={{2,0},{4,2},{6,4},{8,6},{10,8},{12,10},{14,12},{16,14},{18,16},{20... | collective-permute-start | bytes 393224 | tf_op jit(solution)/shard_map/ppermute | solution.py:30
  146.0 11.4 %collective-permute-start.13 = (f32[8,8,8,1]{3,1,2,0:T(8,128)S(1)}, f32[8,8,8,1]{3,1,2,0:T(8,128)S(1)}, u32[]{:S(2)}, u32[]{:S(2)}) collective-permute-start(f32[8,8,8,1]{3,1,2,0:T(8,128)S(1)} %slice.170), channel_id=1, source_target_pairs={{0,128},{128,256},{256,384},{384,0},{1,129},{129,257},{257,385},{3... | collective-permute-start | bytes 6152 | tf_op jit(solution)/shard_map/ppermute | solution.py:24
  166.9 68.3 %copy-start.5 = (f32[8]{0:T(128)S(1)}, f32[8]{0:T(128)}, u32[]{:S(2)}) copy-start(f32[8]{0:T(128)} %param.21) | copy-start | bytes 100
Sparse Core Ops, SparseCore 0:
  169.0 66.2 all-reduce.1
